TPU v7x, 32 devices: a whole 2x2x4 slice. The times are simulated.
32 devices in a mesh: len: 2 (over core), wid: 4 (over y, x), hgt: 4 (over z).
Axes of the slice: x: 2, y: 2, z: 4, core: 2. Of those that a mesh axis runs over, the one named last changes fastest.
Arguments:
- e_field: float32 [3, 32, 128, 512], P(None, 'len', 'wid', 'hgt'), may hold values from -6 to 6
- h_field: float32 [3, 32, 128, 512], P(None, 'len', 'wid', 'hgt'), may hold values from -6 to 6
- material: int32 [32, 128, 512], P('len', 'wid', 'hgt'), may hold values from 0 to 15
- permittivity: float32 [16], replicated, may hold values from 1 to 10
- line_volts: float32 [16, 65536], P(None, ('len', 'wid', 'hgt')), may hold values from -6 to 6
- line_amps: float32 [16, 65536], P(None, ('len', 'wid', 'hgt')), may hold values from -6 to 6
- coupling: float32 [16, 65536], P(None, ('len', 'wid', 'hgt')), may hold values from -3 to 3
- seg_brick: int32 [65536], P(('len', 'wid', 'hgt')), may hold values from 0 to 31, as said below
- seg_cell: int32 [65536], P(('len', 'wid', 'hgt')), may hold values from 0 to 65535
- seg_axis: int32 [65536], P(('len', 'wid', 'hgt')), may hold values from 0 to 2
- bundle_type: int32 [65536], P(('len', 'wid', 'hgt')), may hold values from 0 to 7
- path_lengths: int32 [32, 64], P(('len', 'wid', 'hgt')), may hold values from 1 to 64, 2048 in all within a row
- inv_induct: float32 [8, 16, 16], replicated, may hold values from -0.2 to 1.3, as said below
- inv_capac: float32 [8, 16, 16], replicated, may hold values from -0.2 to 1.3, as said below
Outputs:
- e_final: float32 [3, 32, 128, 512], P(None, 'len', 'wid', 'hgt')
- h_final: float32 [3, 32, 128, 512], P(None, 'len', 'wid', 'hgt')
- volts_final: float32 [16, 65536], P(None, ('len', 'wid', 'hgt'))
- amps_final: float32 [16, 65536], P(None, ('len', 'wid', 'hgt'))
Inputs may be any that keep to these rules, and one draw needn't show every extreme that they name: `seg_brick`: in each aligned block of 2048 entries (one owner's segments) no brick is named more than 160 times, and in every draw one brick is named exactly 160 times in every block. `inv_induct`: each 16 x 16 block is symmetric. `inv_capac`: each 16 x 16 block is symmetric.
All inputs are finite; a program needn't handle non-finite values.
Results may differ from a plain program's by a relative error of at most 0.0003.
Values sent between devices are 32-bit elements; how exact they have to be, the bound alone decides.
A program may use at most 64 MiB of HBM per device.

v0:
```python
import functools

import jax
import jax.numpy as jnp
from jax import lax
from jax.experimental import pallas as pl
from jax.experimental.pallas import tpu as pltpu
from jax.sharding import PartitionSpec as P

ITERS = 4
AXES = ("len", "wid", "hgt")

courant = 0.5
line_step = 0.5
inject_gain = 0.25


def halves(values):
    high = lax.reduce_precision(values, exponent_bits=8, mantissa_bits=7)
    low = values - high
    return high.astype(jnp.bfloat16), low.astype(jnp.bfloat16)


def product(a, b, a_dim, b_dim):
    return lax.dot_general(
        a, b, (((a_dim,), (b_dim,)), ((), ())), preferred_element_type=jnp.float32
    )


def one_hot(indices, size):
    rows = lax.broadcasted_iota(jnp.int32, (size, indices.shape[0]), 0)
    return rows == indices[None, :]


def ranks_in_brick(in_brick):
    devices, count = in_brick.shape
    grouped = in_brick.astype(jnp.bfloat16).reshape(devices, count // 128, 128)
    lane = jnp.arange(128, dtype=jnp.int32)
    before = (lane[:, None] < lane[None, :]).astype(jnp.bfloat16)
    within = product(grouped, before, 2, 0)
    totals = jnp.sum(grouped.astype(jnp.float32), axis=2)
    block = jnp.arange(count // 128, dtype=jnp.int32)
    earlier = (block[:, None] < block[None, :]).astype(jnp.float32)
    ahead = jnp.sum(totals[:, :, None] * earlier[None], axis=1)
    counts = (within + ahead[:, :, None]).reshape(devices, count)
    return jnp.sum(jnp.where(in_brick, counts, 0.0), axis=0).astype(jnp.int32)


def path_masks(lengths_row, count):
    path_ends = jnp.cumsum(lengths_row)
    path_starts = path_ends - lengths_row
    position = jnp.arange(count, dtype=jnp.int32)
    is_last = jnp.any(position[None, :] == (path_ends - 1)[:, None], axis=0)
    is_first = jnp.any(position[None, :] == path_starts[:, None], axis=0)
    return (
        jnp.where(is_last, 0.0, 1.0).astype(jnp.float32),
        jnp.where(is_first, 0.0, 1.0).astype(jnp.float32),
    )


def type_table(table):
    kinds, rows, columns = table.shape
    flat = jnp.transpose(table, (1, 0, 2)).reshape(rows, kinds * columns)
    high, low = halves(flat)
    return jnp.concatenate(
        [
            jnp.concatenate([high, high], axis=1),
            jnp.concatenate([low, jnp.zeros_like(low)], axis=1),
        ],
        axis=0,
    )


MESH = pl.DeviceIdType.MESH
CHUNK = 512


def split(values):
    high = values.astype(jnp.bfloat16)
    return high, (values - high.astype(jnp.float32)).astype(jnp.bfloat16)


def apply_types(table, operand, kind_mask):
    parts = [
        jnp.concatenate([part] * (kind_mask.shape[0] // operand.shape[0]), axis=0) * kind_mask
        for part in split(operand)
    ]
    result = product(table, jnp.concatenate(parts, axis=0), 1, 0)
    return result[: operand.shape[0]] + result[operand.shape[0] :]


def kernel(
    sizes,
    full,
    group,
    e_in,
    h_in,
    coeff,
    rows_of,
    z_of,
    brick_hot,
    pos_hot,
    kind_mask,
    not_last,
    not_first,
    volts_in,
    amps_in,
    coupling,
    induct_table,
    capac_table,
    e_out,
    h_out,
    volts,
    amps,
    e_all,
    h_all,
    row_hot,
    e_turned,
    z_parts,
    flat,
    sample_send,
    sample_recv,
    drive_send,
    drive_recv,
    ey_send,
    ey_halo,
    ez_send,
    ez_halo,
    hy_send,
    hy_halo,
    hz_send,
    hz_halo,
    face_send_sem,
    face_recv_sem,
    a2a_send_sem,
    a2a_recv_sem,
):
    axes = ("len", "wid", "hgt")
    place = [lax.axis_index(axis) for axis in axes]
    me = (place[0] * sizes[1] + place[1]) * sizes[2] + place[2]
    devices = sizes[0] * sizes[1] * sizes[2]
    _, rows_x, rows_y, rows_z = e_in.shape
    rows = 3 * rows_x * rows_y
    slots = rows_of.shape[1]
    conductors, count = volts.shape

    def device(number):
        upper = lax.div(number, sizes[2])
        return (lax.div(upper, sizes[1]), lax.rem(upper, sizes[1]), lax.rem(number, sizes[2]))

    for halo in (ey_halo, ez_halo, hy_halo, hz_halo):
        halo[...] = jnp.zeros(halo.shape, jnp.float32)
    e_all[:, rows_x] = jnp.zeros((3, rows_y, rows_z), jnp.float32)
    h_all[:, 0] = jnp.zeros((3, rows_y, rows_z), jnp.float32)

    barrier = pltpu.get_barrier_semaphore()

    def greet(step, carry):
        other = lax.rem(me + step, devices)
        pl.semaphore_signal(barrier, inc=1, device_id=device(other), device_id_type=MESH)
        return carry

    lax.fori_loop(1, devices, greet, 0)

    e_all[:, :rows_x] = e_in[...]
    h_all[:, 1:] = h_in[...]
    volts[...] = volts_in[...]
    amps[...] = amps_in[...]

    def mark(step, carry):
        base = pl.multiple_of(step * 16, 16)
        number = lax.broadcasted_iota(jnp.int32, (16, CHUNK), 0) + base
        for start in range(0, slots, CHUNK):
            hit = rows_of[:, start : start + CHUNK] == number
            row_hot[pl.ds(base, 16), start : start + CHUNK] = jnp.where(hit, 1.0, 0.0).astype(
                jnp.bfloat16
            )
        return carry

    lax.fori_loop(0, rows // 16, mark, 0)
    pl.semaphore_wait(barrier, devices - 1)

    def faces(sources, targets, upward, first_sem):
        found = []
        for axis in range(3):
            target = list(place)
            if upward:
                has_next, has_previous = place[axis] < sizes[axis] - 1, place[axis] > 0
                target[axis] = jnp.minimum(place[axis] + 1, sizes[axis] - 1)
            else:
                has_next, has_previous = place[axis] > 0, place[axis] < sizes[axis] - 1
                target[axis] = jnp.maximum(place[axis] - 1, 0)
            copy = pltpu.make_async_remote_copy(
                src_ref=sources[axis],
                dst_ref=targets[axis],
                send_sem=face_send_sem.at[first_sem + axis],
                recv_sem=face_recv_sem.at[first_sem + axis],
                device_id=tuple(target),
                device_id_type=MESH,
            )
            found.append((copy, has_next, has_previous))
        return found

    def start_faces(copies):
        for copy, has_next, _ in copies:
            pl.when(has_next)(copy.start)

    def finish_sends(copies):
        for copy, has_next, _ in copies:
            pl.when(has_next)(copy.wait_send)

    def finish_recvs(copies):
        for copy, _, has_previous in copies:
            pl.when(has_previous)(copy.wait_recv)

    e_copies = faces(
        (e_all.at[pl.ds(1, 2), 0], ey_send, ez_send),
        (e_all.at[pl.ds(1, 2), rows_x], ey_halo, ez_halo),
        False,
        0,
    )
    h_copies = faces(
        (h_all.at[pl.ds(1, 2), rows_x], hy_send, hz_send),
        (h_all.at[pl.ds(1, 2), 0], hy_halo, hz_halo),
        True,
        3,
    )

    def exchange(send, recv, which, fill):
        recv[me] = fill(me)

        def one(step, carry):
            other = lax.rem(me + step, devices)
            send[other] = fill(other)
            pltpu.make_async_remote_copy(
                src_ref=send.at[other],
                dst_ref=recv.at[me],
                send_sem=a2a_send_sem.at[which],
                recv_sem=a2a_recv_sem.at[which],
                device_id=device(other),
                device_id_type=MESH,
            ).start()
            return carry

        lax.fori_loop(1, devices, one, 0)

    def arrivals(ref, sem):
        view = ref.at[pl.ds(0, devices - 1)]
        pltpu.make_async_copy(view, view, sem).wait()

    lane = lax.broadcasted_iota(jnp.int32, (rows_y, rows_z), 1)
    line = lax.broadcasted_iota(jnp.int32, (rows_y, rows_z), 0)

    def pack(ref, first, index, source_lane):
        packed = jnp.zeros((rows_y, rows_z), jnp.float32)
        for comp in range(2):
            for i in range(rows_x):
                spot = comp * rows_x + i
                turned = pltpu.roll(ref[comp, first + i], (spot - source_lane) % rows_z, 1)
                packed = jnp.where(lane == spot, turned, packed)
        index[...] = packed

    def step(_, carry):
        for comp in range(2):
            for i in range(rows_x):
                ey_send[comp, i : i + 1] = e_all[2 * comp, i, 0:1]
        pack(e_all, 0, ez_send, 0)
        start_faces(e_copies)

        for comp in range(3):
            turned = e_all[comp, :rows_x].reshape(rows_x * rows_y, rows_z).T
            high, low = split(turned)
            at = comp * rows_x * rows_y
            e_turned[:rows_z, at : at + rows_x * rows_y] = high
            e_turned[rows_z:, at : at + rows_x * rows_y] = low

        def find(part, carry):
            at = pl.multiple_of(part * CHUNK, CHUNK)
            found = product(e_turned[...], row_hot[:, pl.ds(at, CHUNK)], 1, 0)
            number = lax.broadcasted_iota(jnp.int32, (rows_z, CHUNK), 0)
            hit = z_of[:, pl.ds(at, CHUNK)] == number
            value = jnp.where(hit, found[:rows_z] + found[rows_z:], 0.0)
            flat[:, pl.ds(at, CHUNK)] = jnp.sum(value, axis=0, keepdims=True)
            return carry

        lax.fori_loop(0, slots // CHUNK, find, 0)

        def samples_for(other):
            numbers = [part * devices + other for part in range(full)]
            if group:
                numbers.append(full * devices + lax.div(other, group))
            found = [flat[:, pl.ds(pl.multiple_of(n * 128, 128), 128)] for n in numbers]
            return jnp.concatenate(found, axis=1)

        exchange(sample_send, sample_recv, 0, samples_for)

        finish_recvs(e_copies)

        def magnetic(i, carry):
            ex, ey, ez = (e_all[comp, i] for comp in range(3))

            def along_y(value, slot):
                row = ey_halo[slot, pl.ds(i, 1)]
                return jnp.where(line == rows_y - 1, row, pltpu.roll(value, rows_y - 1, 0)) - value

            def along_z(value, slot):
                halo = pltpu.roll(ez_halo[...], rows_z - 1 - slot * rows_x - i, 1)
                return jnp.where(lane == rows_z - 1, halo, pltpu.roll(value, rows_z - 1, 1)) - value

            h_all[0, i + 1] = h_all[0, i + 1] - courant * (along_y(ez, 1) - along_z(ey, 1))
            h_all[1, i + 1] = h_all[1, i + 1] - courant * (
                along_z(ex, 0) - (e_all[2, i + 1] - ez)
            )
            h_all[2, i + 1] = h_all[2, i + 1] - courant * (
                (e_all[1, i + 1] - ey) - along_y(ex, 0)
            )
            return carry

        lax.fori_loop(0, rows_x, magnetic, 0)
        for comp in range(2):
            for i in range(rows_x):
                hy_send[comp, i : i + 1] = h_all[2 * comp, i + 1, rows_y - 1 : rows_y]
        pack(h_all, 1, hz_send, rows_z - 1)
        start_faces(h_copies)

        arrivals(sample_recv, a2a_recv_sem.at[0])
        returned = jnp.concatenate(split(sample_recv[:, 0, :]), axis=0)
        tangents = []
        for start in range(0, count, CHUNK):
            hot = brick_hot[:, start : start + CHUNK]
            by_pos = product(returned, jnp.concatenate([hot, hot], axis=0), 0, 0)
            kept = by_pos * pos_hot[:, start : start + CHUNK].astype(jnp.float32)
            tangents.append(jnp.sum(kept, axis=0, keepdims=True))
        tangent = jnp.concatenate(tangents, axis=1)
        now = volts[...]
        ahead = pltpu.roll(now, count - 1, 1) * not_last[...]
        drive = ahead - now - coupling[...] * tangent
        amps_now = amps[...] - line_step * apply_types(induct_table[...], drive, kind_mask[...])
        amps[...] = amps_now
        common = inject_gain * jnp.sum(coupling[...] * amps_now, axis=0, keepdims=True)
        weighed = jnp.concatenate([brick_hot[...] * part for part in split(common)], axis=0)
        outgoing = product(weighed, pos_hot[...], 1, 1)
        finish_sends(e_copies)
        arrivals(sample_send, a2a_send_sem.at[0])
        drive_send[:, 0, :] = outgoing[:devices] + outgoing[devices:]
        exchange(drive_send, drive_recv, 1, lambda other: drive_send[other])

        behind = pltpu.roll(amps_now, 1, 1) * not_first[...]
        volts[...] = now - line_step * apply_types(
            capac_table[...], amps_now - behind, kind_mask[...]
        )

        finish_recvs(h_copies)

        def electric(i, carry):
            hx, hy, hz = (h_all[comp, i + 1] for comp in range(3))

            def along_y(value, slot):
                row = hy_halo[slot, pl.ds(i, 1)]
                return value - jnp.where(line == 0, row, pltpu.roll(value, 1, 0))

            def along_z(value, slot):
                shift = lax.rem(2 * rows_z - slot * rows_x - i, rows_z)
                halo = pltpu.roll(hz_halo[...], shift, 1)
                return value - jnp.where(lane == 0, halo, pltpu.roll(value, 1, 1))

            gain = coeff[i]
            e_all[0, i] = e_all[0, i] + gain * (along_y(hz, 1) - along_z(hy, 1))
            e_all[1, i] = e_all[1, i] + gain * (along_z(hx, 0) - (hz - h_all[2, i]))
            e_all[2, i] = e_all[2, i] + gain * ((hy - h_all[1, i]) - along_y(hx, 0))
            return carry

        lax.fori_loop(0, rows_x, electric, 0)

        arrivals(drive_recv, a2a_recv_sem.at[1])
        number = lax.broadcasted_iota(jnp.int32, (rows_z, 128), 0)
        for block in range(slots // 128):
            if block < full * devices:
                part, other = divmod(block, devices)
                values = drive_recv[other, :, part * 128 : part * 128 + 128]
            else:
                first = (block - full * devices) * group
                values = drive_recv[first, :, full * 128 :]
                for other in range(first + 1, first + group):
                    values = values + drive_recv[other, :, full * 128 :]
            hit = z_of[:, block * 128 : block * 128 + 128] == number
            high, low = split(values)
            for which, part in enumerate((high, low)):
                z_parts[which * rows_z : (which + 1) * rows_z, block * 128 : block * 128 + 128] = (
                    jnp.where(hit, part.astype(jnp.float32), 0.0).astype(jnp.bfloat16)
                )

        def inject(part, carry):
            at = pl.multiple_of(part * rows_y * 8, rows_y * 8)
            added = product(row_hot[pl.ds(at, rows_y * 8)], z_parts[...], 1, 1)
            added = (added[:, :rows_z] + added[:, rows_z:]).reshape(8, rows_y, rows_z)
            comp = lax.div(part, rows_x // 8)
            first = lax.rem(part, rows_x // 8) * 8
            e_all[comp, pl.ds(first, 8)] = (
                e_all[comp, pl.ds(first, 8)] - coeff[pl.ds(first, 8)] * added
            )
            return carry

        lax.fori_loop(0, rows // (rows_y * 8), inject, 0)
        finish_sends(h_copies)
        arrivals(drive_send, a2a_send_sem.at[1])
        return carry

    lax.fori_loop(0, ITERS, step, 0)
    e_out[...] = e_all[:, :rows_x]
    h_out[...] = h_all[:, 1:]


def shards(
    e_field,
    h_field,
    material,
    permittivity,
    line_volts,
    line_amps,
    coupling,
    seg_brick,
    seg_cell,
    seg_axis,
    bundle_type,
    path_lengths,
    inv_induct,
    inv_capac,
):
    sizes = tuple(lax.axis_size(axis) for axis in AXES)
    devices = sizes[0] * sizes[1] * sizes[2]
    me = lax.axis_index(AXES)
    conductors, seg_count = line_volts.shape
    capacity = seg_count // devices * 5 // 2
    full, rest = divmod(capacity, 128)
    share = 1
    while share < rest:
        share *= 2
    group = 128 // share if rest else 0
    width = 128 * (full + (1 if rest else 0))
    rows_x, rows_y, rows_z = e_field.shape[1:]
    rows = 3 * rows_x * rows_y
    coeff = jnp.zeros(material.shape, jnp.float32)
    for material_id in range(permittivity.shape[0]):
        coeff = jnp.where(material == material_id, courant / permittivity[material_id], coeff)

    in_brick = one_hot(seg_brick, devices)
    rank = ranks_in_brick(in_brick)
    pos = rank
    if rest:
        pos = jnp.where(rank >= full * 128, rank + share * (me % group), rank)
    pos_hot = one_hot(pos, width).astype(jnp.bfloat16)
    row = seg_axis * (rows_x * rows_y) + seg_cell // rows_z
    pieces = (seg_cell % rows_z + 1, row % 256, row // 256)
    placed = jnp.concatenate([jnp.where(in_brick, piece[None, :], 0) for piece in pieces], axis=0)
    placed = product(placed.astype(jnp.bfloat16), pos_hot, 1, 1).astype(jnp.int32)
    wanted = (
        placed[:devices] + placed[devices : 2 * devices] * 256 + placed[2 * devices :] * 65536
    )
    asked = lax.all_to_all(wanted, AXES, split_axis=0, concat_axis=0, tiled=True)
    lists = [asked[:, part * 128 : part * 128 + 128] for part in range(full)]
    if rest:
        lists.append(asked[:, full * 128 :].reshape(devices // group, group, 128).sum(axis=1))
    asked = jnp.concatenate(lists, axis=0).reshape(1, -1)
    slots = asked.shape[1]
    kind_mask = jnp.repeat(one_hot(bundle_type, inv_induct.shape[0]), conductors, axis=0)
    not_last, not_first = path_masks(path_lengths[0], seg_count)

    field = (rows_x, rows_y, rows_z)
    swap = pltpu.VMEM((devices, 1, width), jnp.float32)
    y_face = pltpu.VMEM((2, rows_x, rows_z), jnp.float32)
    z_face = pltpu.VMEM((rows_y, rows_z), jnp.float32)
    return tuple(
        pl.pallas_call(
            functools.partial(kernel, sizes, full, group),
            out_shape=[
                jax.ShapeDtypeStruct(e_field.shape, jnp.float32),
                jax.ShapeDtypeStruct(h_field.shape, jnp.float32),
                jax.ShapeDtypeStruct(line_volts.shape, jnp.float32),
                jax.ShapeDtypeStruct(line_amps.shape, jnp.float32),
            ],
            in_specs=[pl.BlockSpec(memory_space=pltpu.VMEM)] * 15,
            out_specs=[pl.BlockSpec(memory_space=pltpu.VMEM)] * 4,
            scratch_shapes=[
                pltpu.VMEM((3, rows_x + 1, rows_y, rows_z), jnp.float32),
                pltpu.VMEM((3, rows_x + 1, rows_y, rows_z), jnp.float32),
                pltpu.VMEM((rows, slots), jnp.bfloat16),
                pltpu.VMEM((2 * rows_z, rows), jnp.bfloat16),
                pltpu.VMEM((2 * rows_z, slots), jnp.bfloat16),
                pltpu.VMEM((1, slots), jnp.float32),
                swap,
                swap,
                swap,
                swap,
                y_face,
                y_face,
                z_face,
                z_face,
                y_face,
                y_face,
                z_face,
                z_face,
                pltpu.SemaphoreType.DMA((6,)),
                pltpu.SemaphoreType.DMA((6,)),
                pltpu.SemaphoreType.DMA((2,)),
                pltpu.SemaphoreType.DMA((2,)),
            ],
            compiler_params=pltpu.CompilerParams(
                collective_id=0, has_side_effects=True, vmem_limit_bytes=56 * 1024 * 1024
            ),
            cost_estimate=pl.CostEstimate(
                flops=32 * rows * slots * rows_z, bytes_accessed=8 * 1024 * 1024, transcendentals=0
            ),
        )(
            e_field,
            h_field,
            coeff,
            asked // 256,
            asked % 256 - 1,
            in_brick.astype(jnp.bfloat16),
            pos_hot,
            kind_mask.astype(jnp.bfloat16),
            not_last[None, :],
            not_first[None, :],
            line_volts,
            line_amps,
            coupling,
            type_table(inv_induct),
            type_table(inv_capac),
        )
    )


def solution(mesh):
    return jax.shard_map(
        shards,
        mesh=mesh,
        in_specs=(
            P(None, "len", "wid", "hgt"),
            P(None, "len", "wid", "hgt"),
            P("len", "wid", "hgt"),
            P(),
            P(None, ("len", "wid", "hgt")),
            P(None, ("len", "wid", "hgt")),
            P(None, ("len", "wid", "hgt")),
            P(("len", "wid", "hgt")),
            P(("len", "wid", "hgt")),
            P(("len", "wid", "hgt")),
            P(("len", "wid", "hgt")),
            P(("len", "wid", "hgt"), None),
            P(),
            P(),
        ),
        out_specs=(
            P(None, "len", "wid", "hgt"),
            P(None, "len", "wid", "hgt"),
            P(None, ("len", "wid", "hgt")),
            P(None, ("len", "wid", "hgt")),
        ),
        check_vma=False,
    )
```

profile of v0, /device:TPU:0, one launch (start us, length us, event | category | flops | bytes accessed | tf_op | source)
XLA Modules:
  0.0 138.5 jit_solution(4375152420253073326)
XLA Ops:
  0.7 0.8 convert_reduce_fusion
  1.5 0.1 copy.33
  1.6 0.1 multiply_reduce_fusion
  1.7 0.1 copy.34
  1.8 1.0 fusion.3
  2.8 0.7 add_select_fusion.1
  3.5 0.8 select_convert_fusion.2
  4.3 0.0 copy-start.5
  4.3 0.5 fusion.4
  4.8 0.0 copy-start.4
  4.8 0.0 copy-start.8
  4.8 0.0 copy-start.9
  4.8 0.0 copy-start.6
  4.8 0.0 copy-start.7
  4.9 0.0 copy-start.1
  4.9 0.6 copy.35
  5.5 7.3 %all-to-all-start = ((s32[32,1,256]{2,1,0:T(1,128)}), s32[32,1,256]{2,1,0:T(1,128)S(1)}, u32[]{:S(2)}, u32[]{:S(2)}) async-start(s32[32,1,256]{2,1,0:T(1,128)} %copy.35), calls=%async_computation | async-start | bytes 65536 | tf_op jit(solution)/shard_map/all_to_all | solution.py:460
  12.8 0.0 copy-done.5
  12.8 0.7 fusion.14.brick_hot
  13.5 1.2 fusion.pos_hot
  14.7 0.0 copy-done.4
  14.7 0.7 fusion.38
  26.0 0.0 copy-done.8
  26.0 0.0 copy-done.9
  26.0 0.1 copy.36
  26.1 0.1 reduce-window.7
  26.2 0.1 reduce.1
  26.3 0.2 fusion.6
  26.6 0.6 broadcast_select_fusion.1
  27.2 0.6 broadcast_select_fusion
  27.8 0.0 copy-done.6
  27.8 0.1 reshape.302
  27.9 0.0 copy-done.7
  27.9 0.1 reshape.303
  28.0 0.0 copy-done.1
  28.0 1.0 select_select_fusion.coeff
  29.0 0.6 fusion.25
  29.6 0.0 all-to-all-done
  29.7 0.7 fusion.24
  30.4 0.7 and_select_fusion.1.rows_of
  31.0 0.8 broadcast_in_dim.134
  31.9 102.1 %shard_map.165 = (f32[3,16,32,128]{3,2,1,0:T(8,128)}, f32[3,16,32,128]{3,2,1,0:T(8,128)}, f32[16,2048]{1,0:T(8,128)}, f32[16,2048]{1,0:T(8,128)}) custom-call(f32[3,16,32,128]{3,2,1,0:T(8,128)} %e_in.1, f32[3,16,32,128]{3,2,1,0:T(8,128)} %h_in.1, f32[16,32,128]{2,1,0:T(8,128)} %select_select_fusion.coeff, s32[1,5120]{1,0:T(1,128)} %and_select_fusion.1.rows_of, ...), custom_call_target="tpu_custom_call" | custom-call | flops 32212254720 | bytes 8388608 | tf_op jit(solution)/shard_map/pallas_call | solution.py:474
  134.0 0.0 copy-start
  134.0 2.1 %copy.46 = f32[3,16,32,128]{3,2,1,0:T(8,128)} copy(f32[3,16,32,128]{3,2,1,0:T(8,128)} %get-tuple-element.44) | data formatting | bytes 1572864
  136.1 0.0 copy-done
  136.1 0.0 copy-start.3
  136.1 0.0 copy-start.2
  136.1 0.9 copy.47
  137.0 0.1 copy-done.3
  137.1 0.7 copy.48
  137.8 0.0 copy-done.2
  137.8 0.7 copy.49
  (13 shorter events, 0.1 us)
Async XLA Ops:
  4.3 8.6 %copy-start.5 = (s32[2048]{0:T(1024)S(1)}, s32[2048]{0:T(1024)}, u32[]{:S(2)}) copy-start(s32[2048]{0:T(1024)} %param.21) | copy-start | bytes 24580
  4.8 10.0 %copy-start.4 = (f32[16]{0:T(128)S(1)}, f32[16]{0:T(128)}, u32[]{:S(2)}) copy-start(f32[16]{0:T(128)} %param.17) | copy-start | bytes 196
  4.8 21.2 %copy-start.8 = (s32[2048]{0:T(1024)S(1)}, s32[2048]{0:T(1024)}, u32[]{:S(2)}) copy-start(s32[2048]{0:T(1024)} %param.24) | copy-start | bytes 24580
  4.8 21.2 %copy-start.9 = (s32[1,64]{1,0:T(1,128)S(1)}, s32[1,64]{1,0:T(1,128)}, u32[]{:S(2)}) copy-start(s32[1,64]{1,0:T(1,128)} %param.25) | copy-start | bytes 772
  4.8 22.9 %copy-start.6 = (f32[8,16,16]{2,1,0:T(8,128)S(1)}, f32[8,16,16]{2,1,0:T(8,128)}, u32[]{:S(2)}) copy-start(f32[8,16,16]{2,1,0:T(8,128)} %param.26) | copy-start | bytes 24580
  4.8 23.1 %copy-start.7 = (f32[8,16,16]{2,1,0:T(8,128)S(1)}, f32[8,16,16]{2,1,0:T(8,128)}, u32[]{:S(2)}) copy-start(f32[8,16,16]{2,1,0:T(8,128)} %param.27) | copy-start | bytes 24580
  4.9 23.1 %copy-start.1 = (s32[16,32,128]{2,1,0:T(8,128)S(1)}, s32[16,32,128]{2,1,0:T(8,128)}, u32[]{:S(2)}) copy-start(s32[16,32,128]{2,1,0:T(8,128)} %param.16) | copy-start | bytes 786436
  5.5 24.1 %all-to-all-start = ((s32[32,1,256]{2,1,0:T(1,128)}), s32[32,1,256]{2,1,0:T(1,128)S(1)}, u32[]{:S(2)}, u32[]{:S(2)}) async-start(s32[32,1,256]{2,1,0:T(1,128)} %copy.35), calls=%async_computation | async-start | bytes 65536 | tf_op jit(solution)/shard_map/all_to_all | solution.py:460
  134.0 2.1 %copy-start = (f32[3,16,32,128]{3,2,1,0:T(8,128)S(1)}, f32[3,16,32,128]{3,2,1,0:T(8,128)}, u32[]{:S(2)}) copy-start(f32[3,16,32,128]{3,2,1,0:T(8,128)} %get-tuple-element.45) | copy-start | bytes 2359300
  136.1 1.0 copy-start.3
  136.1 1.7 %copy-start.2 = (f32[16,2048]{1,0:T(8,128)S(1)}, f32[16,2048]{1,0:T(8,128)}, u32[]{:S(2)}) copy-start(f32[16,2048]{1,0:T(8,128)} %get-tuple-element.47) | copy-start | bytes 393220
where the time goes:
time: 139 us; the launch traced here: 138 us
  Pallas kernels  102 us (73%)
  between operations  11.4 us (8%)
  other arithmetic  8.97 us (6%)
  starting transfers between devices  7.3 us (5%)
  local copies, waits for them, and re-layouts  7.15 us (5%)
  matrix products  1.48 us (1%)
    pallas_call x1, Pallas kernels, shards(): pl.pallas_call(functools.partial(kernel, sizes, full, group), out_shape=[...  102 us
    all_to_all x1, starting transfers between devices, shards(): lax.all_to_all(wanted, AXES, split_axis=0, concat_axis=0, tiled=True)  7.3 us
    unnamed x25, local copies, waits for them, and re-layouts  4.5 us
  transfers between devices with their start and end apart: 1, of which 0 were waited for; matrix products, arithmetic and copies ran while one was open for 4% of the time, Pallas kernels for 0%

commit v1 on v0

--- a/solution.py
+++ b/solution.py
@@ -73,6 +73,8 @@
 
 MESH = pl.DeviceIdType.MESH
 CHUNK = 512
+FOLD = 1
+INJECT = 1
 
 
 def split(values):
@@ -95,9 +97,9 @@
     group,
     e_in,
     h_in,
-    coeff,
-    rows_of,
-    z_of,
+    material,
+    gains,
+    wanted,
     brick_hot,
     pos_hot,
     kind_mask,
@@ -114,6 +116,9 @@
     amps,
     e_all,
     h_all,
+    coeff,
+    rows_of,
+    z_of,
     row_hot,
     e_turned,
     z_parts,
@@ -140,8 +145,9 @@
     me = (place[0] * sizes[1] + place[1]) * sizes[2] + place[2]
     devices = sizes[0] * sizes[1] * sizes[2]
     _, rows_x, rows_y, rows_z = e_in.shape
-    rows = 3 * rows_x * rows_y
-    slots = rows_of.shape[1]
+    rows, slots = row_hot.shape
+    span_x = rows_x // FOLD
+    deep = FOLD * rows_z
     conductors, count = volts.shape
 
     def device(number):
@@ -161,24 +167,6 @@
         return carry
 
     lax.fori_loop(1, devices, greet, 0)
-
-    e_all[:, :rows_x] = e_in[...]
-    h_all[:, 1:] = h_in[...]
-    volts[...] = volts_in[...]
-    amps[...] = amps_in[...]
-
-    def mark(step, carry):
-        base = pl.multiple_of(step * 16, 16)
-        number = lax.broadcasted_iota(jnp.int32, (16, CHUNK), 0) + base
-        for start in range(0, slots, CHUNK):
-            hit = rows_of[:, start : start + CHUNK] == number
-            row_hot[pl.ds(base, 16), start : start + CHUNK] = jnp.where(hit, 1.0, 0.0).astype(
-                jnp.bfloat16
-            )
-        return carry
-
-    lax.fori_loop(0, rows // 16, mark, 0)
-    pl.semaphore_wait(barrier, devices - 1)
 
     def faces(sources, targets, upward, first_sem):
         found = []
@@ -260,6 +248,52 @@
                 packed = jnp.where(lane == spot, turned, packed)
         index[...] = packed
 
+    def block_values(ref, block):
+        if block < full * devices:
+            part, other = divmod(block, devices)
+            return ref[other, :, part * 128 : part * 128 + 128]
+        first = (block - full * devices) * group
+        values = ref[first, :, full * 128 :]
+        for other in range(first + 1, first + group):
+            values = values + ref[other, :, full * 128 :]
+        return values
+
+    pl.semaphore_wait(barrier, devices - 1)
+    exchange(drive_send, drive_recv, 1, lambda other: wanted[other])
+
+    e_all[:, :rows_x] = e_in[...]
+    h_all[:, 1:] = h_in[...]
+    volts[...] = volts_in[...]
+    amps[...] = amps_in[...]
+
+    def fill_coeff(i, carry):
+        kinds = material[i]
+        gain = jnp.zeros((rows_y, rows_z), jnp.float32)
+        for kind in range(gains.shape[0]):
+            gain = jnp.where(kinds == kind, gains[kind : kind + 1], gain)
+        coeff[i] = gain
+        return carry
+
+    lax.fori_loop(0, rows_x, fill_coeff, 0)
+    arrivals(drive_recv, a2a_recv_sem.at[1])
+    for block in range(slots // 128):
+        code = block_values(drive_recv, block).astype(jnp.int32) - 1
+        rows_of[:, block * 128 : block * 128 + 128] = code >> (deep.bit_length() - 1)
+        z_of[:, block * 128 : block * 128 + 128] = code & (deep - 1)
+    arrivals(drive_send, a2a_send_sem.at[1])
+
+    def mark(step, carry):
+        base = pl.multiple_of(step * 16, 16)
+        number = lax.broadcasted_iota(jnp.int32, (16, CHUNK), 0) + base
+        for start in range(0, slots, CHUNK):
+            hit = rows_of[:, start : start + CHUNK] == number
+            row_hot[pl.ds(base, 16), start : start + CHUNK] = jnp.where(hit, 1.0, 0.0).astype(
+                jnp.bfloat16
+            )
+        return carry
+
+    lax.fori_loop(0, rows // 16, mark, 0)
+
     def step(_, carry):
         for comp in range(2):
             for i in range(rows_x):
@@ -268,18 +302,19 @@
         start_faces(e_copies)
 
         for comp in range(3):
-            turned = e_all[comp, :rows_x].reshape(rows_x * rows_y, rows_z).T
-            high, low = split(turned)
-            at = comp * rows_x * rows_y
-            e_turned[:rows_z, at : at + rows_x * rows_y] = high
-            e_turned[rows_z:, at : at + rows_x * rows_y] = low
+            for fold in range(FOLD):
+                part = e_all[comp, fold * span_x : (fold + 1) * span_x]
+                high, low = split(part.reshape(span_x * rows_y, rows_z).T)
+                at = comp * span_x * rows_y
+                e_turned[fold * rows_z : (fold + 1) * rows_z, at : at + span_x * rows_y] = high
+                e_turned[deep + fold * rows_z : deep + (fold + 1) * rows_z, at : at + span_x * rows_y] = low
 
         def find(part, carry):
             at = pl.multiple_of(part * CHUNK, CHUNK)
             found = product(e_turned[...], row_hot[:, pl.ds(at, CHUNK)], 1, 0)
-            number = lax.broadcasted_iota(jnp.int32, (rows_z, CHUNK), 0)
+            number = lax.broadcasted_iota(jnp.int32, (deep, CHUNK), 0)
             hit = z_of[:, pl.ds(at, CHUNK)] == number
-            value = jnp.where(hit, found[:rows_z] + found[rows_z:], 0.0)
+            value = jnp.where(hit, found[:deep] + found[deep:], 0.0)
             flat[:, pl.ds(at, CHUNK)] = jnp.sum(value, axis=0, keepdims=True)
             return carry
 
@@ -373,35 +408,24 @@
         lax.fori_loop(0, rows_x, electric, 0)
 
         arrivals(drive_recv, a2a_recv_sem.at[1])
-        number = lax.broadcasted_iota(jnp.int32, (rows_z, 128), 0)
+        number = lax.broadcasted_iota(jnp.int32, (deep, 128), 0)
         for block in range(slots // 128):
-            if block < full * devices:
-                part, other = divmod(block, devices)
-                values = drive_recv[other, :, part * 128 : part * 128 + 128]
-            else:
-                first = (block - full * devices) * group
-                values = drive_recv[first, :, full * 128 :]
-                for other in range(first + 1, first + group):
-                    values = values + drive_recv[other, :, full * 128 :]
-            hit = z_of[:, block * 128 : block * 128 + 128] == number
+            values = block_values(drive_recv, block)
+            lanes = slice(block * 128, block * 128 + 128)
+            hit = z_of[:, lanes] == number
             high, low = split(values)
-            for which, part in enumerate((high, low)):
-                z_parts[which * rows_z : (which + 1) * rows_z, block * 128 : block * 128 + 128] = (
-                    jnp.where(hit, part.astype(jnp.float32), 0.0).astype(jnp.bfloat16)
-                )
-
-        def inject(part, carry):
-            at = pl.multiple_of(part * rows_y * 8, rows_y * 8)
-            added = product(row_hot[pl.ds(at, rows_y * 8)], z_parts[...], 1, 1)
-            added = (added[:, :rows_z] + added[:, rows_z:]).reshape(8, rows_y, rows_z)
-            comp = lax.div(part, rows_x // 8)
-            first = lax.rem(part, rows_x // 8) * 8
-            e_all[comp, pl.ds(first, 8)] = (
-                e_all[comp, pl.ds(first, 8)] - coeff[pl.ds(first, 8)] * added
-            )
-            return carry
-
-        lax.fori_loop(0, rows // (rows_y * 8), inject, 0)
+            z_parts[:deep, lanes] = jnp.where(hit, high.astype(jnp.float32), 0.0).astype(jnp.bfloat16)
+            z_parts[deep:, lanes] = jnp.where(hit, low.astype(jnp.float32), 0.0).astype(jnp.bfloat16)
+
+        for first in range(0, rows, rows // INJECT):
+            added = product(row_hot[first : first + rows // INJECT], z_parts[...], 1, 1)
+            comps = slice(first * 3 // rows, first * 3 // rows + 3 // INJECT)
+            for fold in range(FOLD):
+                high = added[:, fold * rows_z : (fold + 1) * rows_z]
+                low = added[:, deep + fold * rows_z : deep + (fold + 1) * rows_z]
+                change = (high + low).reshape(3 // INJECT, span_x, rows_y, rows_z)
+                planes = slice(fold * span_x, (fold + 1) * span_x)
+                e_all[comps, planes] = e_all[comps, planes] - coeff[planes] * change
         finish_sends(h_copies)
         arrivals(drive_send, a2a_send_sem.at[1])
         return carry
@@ -439,30 +463,24 @@
     group = 128 // share if rest else 0
     width = 128 * (full + (1 if rest else 0))
     rows_x, rows_y, rows_z = e_field.shape[1:]
-    rows = 3 * rows_x * rows_y
-    coeff = jnp.zeros(material.shape, jnp.float32)
-    for material_id in range(permittivity.shape[0]):
-        coeff = jnp.where(material == material_id, courant / permittivity[material_id], coeff)
-
     in_brick = one_hot(seg_brick, devices)
     rank = ranks_in_brick(in_brick)
     pos = rank
     if rest:
         pos = jnp.where(rank >= full * 128, rank + share * (me % group), rank)
     pos_hot = one_hot(pos, width).astype(jnp.bfloat16)
-    row = seg_axis * (rows_x * rows_y) + seg_cell // rows_z
-    pieces = (seg_cell % rows_z + 1, row % 256, row // 256)
+    y_and_z = rows_y * rows_z
+    x_of = seg_cell // y_and_z
+    span_x = rows_x // FOLD
+    row = (seg_axis * span_x + x_of % span_x) * rows_y + seg_cell % y_and_z // rows_z
+    code = (row * FOLD + x_of // span_x) * rows_z + seg_cell % rows_z + 1
+    pieces = (code % 256, code // 256 % 256, code // 65536)
     placed = jnp.concatenate([jnp.where(in_brick, piece[None, :], 0) for piece in pieces], axis=0)
-    placed = product(placed.astype(jnp.bfloat16), pos_hot, 1, 1).astype(jnp.int32)
-    wanted = (
-        placed[:devices] + placed[devices : 2 * devices] * 256 + placed[2 * devices :] * 65536
-    )
-    asked = lax.all_to_all(wanted, AXES, split_axis=0, concat_axis=0, tiled=True)
-    lists = [asked[:, part * 128 : part * 128 + 128] for part in range(full)]
-    if rest:
-        lists.append(asked[:, full * 128 :].reshape(devices // group, group, 128).sum(axis=1))
-    asked = jnp.concatenate(lists, axis=0).reshape(1, -1)
-    slots = asked.shape[1]
+    placed = product(placed.astype(jnp.bfloat16), pos_hot, 1, 1)
+    wanted = placed[:devices] + placed[devices : 2 * devices] * 256 + placed[2 * devices :] * 65536
+    gains = jnp.broadcast_to((courant / permittivity)[:, None], (permittivity.shape[0], rows_z))
+    rows = 3 * span_x * rows_y
+    slots = 128 * (devices * full + (devices // group if rest else 0))
     kind_mask = jnp.repeat(one_hot(bundle_type, inv_induct.shape[0]), conductors, axis=0)
     not_last, not_first = path_masks(path_lengths[0], seg_count)
 
@@ -484,9 +502,12 @@
             scratch_shapes=[
                 pltpu.VMEM((3, rows_x + 1, rows_y, rows_z), jnp.float32),
                 pltpu.VMEM((3, rows_x + 1, rows_y, rows_z), jnp.float32),
+                pltpu.VMEM(field, jnp.float32),
+                pltpu.VMEM((1, slots), jnp.int32),
+                pltpu.VMEM((1, slots), jnp.int32),
                 pltpu.VMEM((rows, slots), jnp.bfloat16),
-                pltpu.VMEM((2 * rows_z, rows), jnp.bfloat16),
-                pltpu.VMEM((2 * rows_z, slots), jnp.bfloat16),
+                pltpu.VMEM((2 * FOLD * rows_z, rows), jnp.bfloat16),
+                pltpu.VMEM((2 * FOLD * rows_z, slots), jnp.bfloat16),
                 pltpu.VMEM((1, slots), jnp.float32),
                 swap,
                 swap,
@@ -514,9 +535,9 @@
         )(
             e_field,
             h_field,
-            coeff,
-            asked // 256,
-            asked % 256 - 1,
+            material,
+            gains,
+            wanted[:, None, :],
             in_brick.astype(jnp.bfloat16),
             pos_hot,
             kind_mask.astype(jnp.bfloat16),

time: 139 us -> 124 us (0.89)
  between operations: 11.4 us -> 0.77 us
  starting transfers between devices: 7.3 us -> 0 us
  Pallas kernels: 102 us -> 104 us
  local copies, waits for them, and re-layouts: 7.15 us -> 8.55 us
    all_to_all x1 -> x0, starting transfers between devices: 7.3 us -> none  [shards(): lax.all_to_all(wanted, AXES, split_axis=0, concat_axis=0, tiled=True)]
    pallas_call x1, Pallas kernels: 102 us -> 104 us  [shards(): pl.pallas_call(functools.partial(kernel, sizes, full, group), out_shape=[...]
    select_n x3 -> x2, other arithmetic: 2.4 us -> 0.77 us  [shards(): pieces = (code % 256, code // 256 % 256, code // 65536)]
    unnamed x25 -> x14, local copies, waits for them, and re-layouts: 4.5 us -> 4.46 us
  transfers between devices with their start and end apart: 1 -> 0, of which waited for: 0 -> 0; matrix products, arithmetic and copies ran while one was open for 4% -> 0% of each run, Pallas kernels for 0% -> 0%
where the time goes in v1:
time: 124 us; the launch traced here: 123 us
  Pallas kernels  104 us (84%)
  local copies, waits for them, and re-layouts  8.55 us (7%)
  other arithmetic  8.01 us (6%)
  matrix products  1.47 us (1%)
    pallas_call x1, Pallas kernels, shards(): pl.pallas_call(functools.partial(kernel, sizes, full, group), out_shape=[...  104 us
    unnamed x14, local copies, waits for them, and re-layouts  4.46 us

profile of v1, /device:TPU:0, one launch (start us, length us, event | category | flops | bytes accessed | tf_op | source)
XLA Modules:
  0.0 123.2 jit_solution(2646890249874476578)
XLA Ops:
  0.6 0.0 copy-start.3
  0.6 0.0 copy-start.4
  0.7 0.7 broadcast_divide_fusion
  1.4 0.7 broadcast_in_dim.69.gains
  2.0 0.8 convert_reduce_fusion
  2.9 0.1 copy.28
  2.9 0.1 multiply_reduce_fusion
  3.1 0.1 copy.29
  3.1 1.0 fusion.3
  4.1 0.8 add_select_fusion.3
  4.9 0.7 fusion.17
  5.6 0.7 copy.30
  6.4 0.1 reduce-window.7
  6.5 0.1 reduce.1
  6.6 0.7 bitcast_subtract_fusion
  7.2 0.2 fusion.5
  7.5 0.6 broadcast_select_fusion.1
  8.1 0.6 broadcast_select_fusion
  8.7 0.9 copy.31
  9.5 0.1 reshape.117
  9.6 0.0 copy-done.4
  9.7 0.1 reshape.118
  9.7 0.6 fusion.22
  10.4 0.0 copy-done.3
  10.4 0.7 fusion.13.brick_hot
  11.0 0.1 select_convert_fusion.2
  11.1 0.5 fusion.1
  11.6 0.6 broadcast_in_dim.75.wanted
  12.3 0.8 broadcast_in_dim.76
  13.1 1.2 fusion.pos_hot
  14.3 104.4 %shard_map.165 = (f32[3,16,32,128]{3,2,1,0:T(8,128)}, f32[3,16,32,128]{3,2,1,0:T(8,128)}, f32[16,2048]{1,0:T(8,128)}, f32[16,2048]{1,0:T(8,128)}) custom-call(f32[3,16,32,128]{3,2,1,0:T(8,128)} %e_in.1, f32[3,16,32,128]{3,2,1,0:T(8,128)} %h_in.1, s32[16,32,128]{2,1,0:T(8,128)} %material.1, f32[16,128]{1,0:T(8,128)} %broadcast_in_dim.69.gains, ...), custom_call_target="tpu_custom_call" | custom-call | flops 32212254720 | bytes 8388608 | tf_op jit(solution)/shard_map/pallas_call | solution.py:492
  118.7 0.0 copy-start
  118.7 2.1 %copy.37 = f32[3,16,32,128]{3,2,1,0:T(8,128)} copy(f32[3,16,32,128]{3,2,1,0:T(8,128)} %get-tuple-element.25) | data formatting | bytes 1572864
  120.9 0.0 copy-done
  120.9 0.0 copy-start.2
  120.9 0.0 copy-start.1
  120.9 0.9 copy.38
  121.8 0.1 copy-done.2
  121.9 0.7 copy.39
  122.5 0.0 copy-done.1
  122.5 0.7 copy.40
  (7 shorter events, 0.1 us)
Async XLA Ops:
  0.6 9.7 %copy-start.3 = (s32[2048]{0:T(1024)S(1)}, s32[2048]{0:T(1024)}, u32[]{:S(2)}) copy-start(s32[2048]{0:T(1024)} %param.21) | copy-start | bytes 24580
  0.6 9.0 %copy-start.4 = (f32[8,16,16]{2,1,0:T(8,128)S(1)}, f32[8,16,16]{2,1,0:T(8,128)}, u32[]{:S(2)}) copy-start(f32[8,16,16]{2,1,0:T(8,128)} %param.27) | copy-start | bytes 24580
  118.7 2.1 %copy-start = (f32[3,16,32,128]{3,2,1,0:T(8,128)S(1)}, f32[3,16,32,128]{3,2,1,0:T(8,128)}, u32[]{:S(2)}) copy-start(f32[3,16,32,128]{3,2,1,0:T(8,128)} %get-tuple-element.26) | copy-start | bytes 2359300
  120.9 1.0 copy-start.2
  120.9 1.7 %copy-start.1 = (f32[16,2048]{1,0:T(8,128)S(1)}, f32[16,2048]{1,0:T(8,128)}, u32[]{:S(2)}) copy-start(f32[16,2048]{1,0:T(8,128)} %get-tuple-element.28) | copy-start | bytes 393220
